TPU v7x, 512 devices: a whole 4x8x8 slice. The times are simulated.
512 devices in a mesh: grp: 16 (over x, z_hi), body: 32 (over y, z_lo, core).
Axes of the slice: x: 4, y: 8, z: 8 (z_hi: 4, z_lo: 2; z = z_hi * 2 + z_lo), core: 2. Of those that a mesh axis runs over, the one named last changes fastest.
Arguments:
- incident: bfloat16 [512, 16, 512], P(('grp', 'body')), may hold values from -6 to 6
- exciting: float32 [512, 16, 512], P(('grp', 'body')), may hold values from -6 to 6
- t_matrices: bfloat16 [512, 2, 256, 256], P(('grp', 'body')), may hold values from -0.1875 to 0.1875
- hankel_rows: bfloat16 [225, 2, 512], replicated, may hold values from -0.046875 to 0.046875
- offsets: int32 [512, 32], P(('grp', 'body')), may hold values from 0 to 224
- lattice_slots: int32 [512], P('grp'), may hold values from 0 to 31, as said below
- up_maps: bfloat16 [512, 2, 256, 512], P(('grp', 'body')), may hold values from -0.0625 to 0.0625
- down_maps: bfloat16 [512, 2, 512, 256], P(('grp', 'body')), may hold values from -0.1875 to 0.1875
- group_maps: bfloat16 [16, 16, 2, 512, 512], P('grp', None, None, 'body'), may hold values from -0.046875 to 0.046875
Outputs:
- updated: float32 [512, 16, 512], P(('grp', 'body'))
Inputs may be any that keep to these rules, and one draw needn't show every extreme that they name: `lattice_slots`: within each group the 32 columns stand at the slots 0 to 31, one column a slot.
All inputs are finite; a program needn't handle non-finite values.
Results may differ from a plain program's by a relative error of at most 0.0034.
Values may be sent and summed in bfloat16 or wider, within the bound.
A program may use at most 64 MiB of HBM per device.

v0:
```python
import math

import jax
import jax.numpy as jnp
from jax import lax
from jax.sharding import PartitionSpec as P


def complex_apply(form, values, real_mats, imag_mats):
    half_width = values.shape[-1] // 2
    real_values = values[..., :half_width]
    imag_values = values[..., half_width:]
    real_out = jnp.einsum(
        form, real_values, real_mats, preferred_element_type=jnp.float32
    ) - jnp.einsum(form, imag_values, imag_mats, preferred_element_type=jnp.float32)
    imag_out = jnp.einsum(
        form, real_values, imag_mats, preferred_element_type=jnp.float32
    ) + jnp.einsum(form, imag_values, real_mats, preferred_element_type=jnp.float32)
    return jnp.concatenate([real_out, imag_out], axis=-1)


def toeplitz_mats(sequences):
    length = sequences.shape[-1] // 2
    repeats = (1,) * (sequences.ndim - 1) + (length,)
    tiled = jnp.tile(sequences, repeats)
    window = tiled[..., length : length + length * (2 * length - 1)]
    return window.reshape(sequences.shape[:-1] + (length, 2 * length - 1))[..., :length]


def local(
    incident,
    exciting,
    t_matrices,
    hankel_rows,
    offsets,
    lattice_slots,
    up_maps,
    down_maps,
    group_maps,
):
    body_index = lax.axis_index("body")
    group_index = lax.axis_index("grp")
    local_count = incident.shape[0]
    scattered = complex_apply("iln,inm->ilm", incident, t_matrices[:, 0], t_matrices[:, 1]).astype(
        jnp.bfloat16
    )
    own_members = body_index * local_count + jnp.arange(local_count, dtype=jnp.int32)
    zero_seq = jnp.zeros((), jnp.bfloat16)
    all_offsets = lax.all_gather(offsets, "body", axis=0, tiled=True)
    group_count = lattice_slots.shape[0]
    own_slots = lax.dynamic_slice_in_dim(lattice_slots, body_index * local_count, local_count, 0)
    table_rows = jnp.take(all_offsets, own_slots, axis=1)
    sequences = jnp.take(hankel_rows, table_rows, axis=0)
    targets = jnp.arange(group_count, dtype=jnp.int32)
    keep = targets[:, None] != own_members[None, :]
    sequences = jnp.where(keep[:, :, None, None], sequences, zero_seq)
    block_rows = math.gcd(group_count, 4)
    sequences = sequences.reshape((group_count // block_rows, block_rows) + sequences.shape[1:])

    def one_block(block_seqs):
        mats = toeplitz_mats(block_seqs)
        return complex_apply("sln,tsnm->tlm", scattered, mats[:, :, 0], mats[:, :, 1])

    terms = lax.map(one_block, sequences)
    totals = lax.psum(terms.reshape((group_count,) + terms.shape[2:]), "body")
    near = lax.dynamic_slice_in_dim(totals, body_index * local_count, local_count, 0)
    partial_value = complex_apply("iln,inq->lq", scattered, up_maps[:, 0], up_maps[:, 1])
    expansion = lax.psum(partial_value, "body").astype(jnp.bfloat16)
    block_width = group_maps.shape[3]
    full_width = group_maps.shape[4]
    real_block = lax.dynamic_slice_in_dim(expansion, body_index * block_width, block_width, 1)
    imag_block = lax.dynamic_slice_in_dim(
        expansion, full_width + body_index * block_width, block_width, 1
    )
    own_block = jnp.concatenate([real_block, imag_block], axis=-1)[None]
    piece = lax.all_gather(own_block, "grp", axis=0, tiled=True)
    width = piece.shape[0]
    sources = jnp.arange(width, dtype=jnp.int32)
    piece = jnp.where((sources != group_index)[:, None, None], piece, zero_seq)
    mats = group_maps[0]
    incoming_part = complex_apply("hln,hnq->lq", piece, mats[:, 0], mats[:, 1])
    incoming = lax.psum(incoming_part, "body").astype(jnp.bfloat16)
    far = complex_apply("lq,iqp->ilp", incoming, down_maps[:, 0], down_maps[:, 1])
    return exciting + near + far


def solution(mesh):
    return jax.shard_map(
        local,
        mesh=mesh,
        in_specs=(
            P(("grp", "body"), None, None),
            P(("grp", "body"), None, None),
            P(("grp", "body"), None, None, None),
            P(),
            P(("grp", "body"), None),
            P("grp"),
            P(("grp", "body"), None, None, None),
            P(("grp", "body"), None, None, None),
            P("grp", None, None, "body", None),
        ),
        out_specs=P(("grp", "body"), None, None),
        check_vma=False,
    )
```

profile of v0, /device:TPU:1, one launch (start us, length us, event | category | flops | bytes accessed | tf_op | source)
XLA Modules:
  0.0 437.1 jit_solution(12570242964982283185)
XLA Ops:
  8.7 1.3 dynamic_slice.16
  12.1 37.1 %all-gather.1 = s32[32,1,32]{2,1,0:T(1,128)S(1)} all-gather(s32[1,1,32]{2,1,0:T(1,128)} %bitcast.159), channel_id=1, replica_groups=mesh['grp'=16,'body'=32] {'body'}, dimensions={0}, use_global_device_ids=true | all-gather | bytes 4224 | tf_op jit(solution)/shard_map/all_gather | solution.py:49
  49.2 1.3 fusion.67
  53.7 119.1 %while.11 = (s32[]{:T(128)}, f32[8,4,16,512]{3,2,1,0:T(8,128)}, bf16[8,4,1,2,512]{4,3,1,2,0:T(2,128)(2,1)S(1)}, bf16[1,16,512]{2,1,0:T(8,128)(2,1)S(1)}, s32[]{:T(128)}) while((s32[]{:T(128)}, f32[8,4,16,512]{3,2,1,0:T(8,128)}, bf16[8,4,1,2,512]{4,3,1,2,0:T(2,128)(2,1)S(1)}, bf16[1,16,512]{2,1,0:T(8,128)(2,1)S(1)}, s32[]{:T(128)}) %tuple.28), condition=%wide.region_1.2_spmd, body=%wide.region_0.1_spmd.sunk | while | flops 33619968 | bytes 17474112 | solution.py:64
  53.9 2.8 tile.14
  56.7 4.4 %slice.219 = bf16[4,1,2,130816]{3,2,0,1:T(2,128)(2,1)} slice(bf16[4,1,2,131072]{3,2,0,1:T(2,128)(2,1)} %tile.14), slice={[0:4], [0:1], [0:2], [256:131072]} | slice | bytes 4186112 | tf_op jit(solution)/shard_map/while/body/eval_jaxpr/slice | solution.py:26
  61.1 6.1 %reshape.288 = bf16[4,1,2,256,511]{4,3,2,0,1:T(8,128)(2,1)S(1)} reshape(bf16[4,1,2,130816]{3,2,0,1:T(2,128)(2,1)} %slice.219) | data formatting | bytes 4186112 | tf_op jit(solution)/shard_map/while/body/eval_jaxpr/reshape | solution.py:27
  68.7 2.8 tile.14
  71.5 4.4 %slice.219 = bf16[4,1,2,130816]{3,2,0,1:T(2,128)(2,1)} slice(bf16[4,1,2,131072]{3,2,0,1:T(2,128)(2,1)} %tile.14), slice={[0:4], [0:1], [0:2], [256:131072]} | slice | bytes 4186112 | tf_op jit(solution)/shard_map/while/body/eval_jaxpr/slice | solution.py:26
  75.9 6.1 %reshape.288 = bf16[4,1,2,256,511]{4,3,2,0,1:T(8,128)(2,1)S(1)} reshape(bf16[4,1,2,130816]{3,2,0,1:T(2,128)(2,1)} %slice.219) | data formatting | bytes 4186112 | tf_op jit(solution)/shard_map/while/body/eval_jaxpr/reshape | solution.py:27
  83.6 2.8 tile.14
  86.4 4.4 %slice.219 = bf16[4,1,2,130816]{3,2,0,1:T(2,128)(2,1)} slice(bf16[4,1,2,131072]{3,2,0,1:T(2,128)(2,1)} %tile.14), slice={[0:4], [0:1], [0:2], [256:131072]} | slice | bytes 4186112 | tf_op jit(solution)/shard_map/while/body/eval_jaxpr/slice | solution.py:26
  90.8 6.1 %reshape.288 = bf16[4,1,2,256,511]{4,3,2,0,1:T(8,128)(2,1)S(1)} reshape(bf16[4,1,2,130816]{3,2,0,1:T(2,128)(2,1)} %slice.219) | data formatting | bytes 4186112 | tf_op jit(solution)/shard_map/while/body/eval_jaxpr/reshape | solution.py:27
  98.5 2.8 tile.14
  101.3 4.4 %slice.219 = bf16[4,1,2,130816]{3,2,0,1:T(2,128)(2,1)} slice(bf16[4,1,2,131072]{3,2,0,1:T(2,128)(2,1)} %tile.14), slice={[0:4], [0:1], [0:2], [256:131072]} | slice | bytes 4186112 | tf_op jit(solution)/shard_map/while/body/eval_jaxpr/slice | solution.py:26
  105.7 6.1 %reshape.288 = bf16[4,1,2,256,511]{4,3,2,0,1:T(8,128)(2,1)S(1)} reshape(bf16[4,1,2,130816]{3,2,0,1:T(2,128)(2,1)} %slice.219) | data formatting | bytes 4186112 | tf_op jit(solution)/shard_map/while/body/eval_jaxpr/reshape | solution.py:27
  113.4 2.8 tile.14
  116.2 4.4 %slice.219 = bf16[4,1,2,130816]{3,2,0,1:T(2,128)(2,1)} slice(bf16[4,1,2,131072]{3,2,0,1:T(2,128)(2,1)} %tile.14), slice={[0:4], [0:1], [0:2], [256:131072]} | slice | bytes 4186112 | tf_op jit(solution)/shard_map/while/body/eval_jaxpr/slice | solution.py:26
  120.6 6.1 %reshape.288 = bf16[4,1,2,256,511]{4,3,2,0,1:T(8,128)(2,1)S(1)} reshape(bf16[4,1,2,130816]{3,2,0,1:T(2,128)(2,1)} %slice.219) | data formatting | bytes 4186112 | tf_op jit(solution)/shard_map/while/body/eval_jaxpr/reshape | solution.py:27
  128.3 2.8 tile.14
  131.1 4.4 %slice.219 = bf16[4,1,2,130816]{3,2,0,1:T(2,128)(2,1)} slice(bf16[4,1,2,131072]{3,2,0,1:T(2,128)(2,1)} %tile.14), slice={[0:4], [0:1], [0:2], [256:131072]} | slice | bytes 4186112 | tf_op jit(solution)/shard_map/while/body/eval_jaxpr/slice | solution.py:26
  135.5 6.1 %reshape.288 = bf16[4,1,2,256,511]{4,3,2,0,1:T(8,128)(2,1)S(1)} reshape(bf16[4,1,2,130816]{3,2,0,1:T(2,128)(2,1)} %slice.219) | data formatting | bytes 4186112 | tf_op jit(solution)/shard_map/while/body/eval_jaxpr/reshape | solution.py:27
  143.1 2.8 tile.14
  145.9 4.4 %slice.219 = bf16[4,1,2,130816]{3,2,0,1:T(2,128)(2,1)} slice(bf16[4,1,2,131072]{3,2,0,1:T(2,128)(2,1)} %tile.14), slice={[0:4], [0:1], [0:2], [256:131072]} | slice | bytes 4186112 | tf_op jit(solution)/shard_map/while/body/eval_jaxpr/slice | solution.py:26
  150.3 6.1 %reshape.288 = bf16[4,1,2,256,511]{4,3,2,0,1:T(8,128)(2,1)S(1)} reshape(bf16[4,1,2,130816]{3,2,0,1:T(2,128)(2,1)} %slice.219) | data formatting | bytes 4186112 | tf_op jit(solution)/shard_map/while/body/eval_jaxpr/reshape | solution.py:27
  158.0 2.8 tile.14
  160.8 4.4 %slice.219 = bf16[4,1,2,130816]{3,2,0,1:T(2,128)(2,1)} slice(bf16[4,1,2,131072]{3,2,0,1:T(2,128)(2,1)} %tile.14), slice={[0:4], [0:1], [0:2], [256:131072]} | slice | bytes 4186112 | tf_op jit(solution)/shard_map/while/body/eval_jaxpr/slice | solution.py:26
  165.2 6.1 %reshape.288 = bf16[4,1,2,256,511]{4,3,2,0,1:T(8,128)(2,1)S(1)} reshape(bf16[4,1,2,130816]{3,2,0,1:T(2,128)(2,1)} %slice.219) | data formatting | bytes 4186112 | tf_op jit(solution)/shard_map/while/body/eval_jaxpr/reshape | solution.py:27
  173.4 102.0 %psum.22 = bf16[16,1024]{1,0:T(8,128)(2,1)S(1)} all-reduce(f32[16,1024]{1,0:T(8,128)S(1)} %pad_maximum_fusion), channel_id=1, replica_groups=mesh['grp'=16,'body'=32] {'body'}, use_global_device_ids=true, to_apply=%region_3.4 | all-reduce | flops 16384 | bytes 98304 | tf_op jit(solution)/shard_map/psum | solution.py:68
  275.6 39.8 %all-gather = bf16[256,32]{1,0:T(8,128)(2,1)S(1)} all-gather(bf16[16,32]{1,0:T(8,128)(2,1)S(1)} %pad_maximum_fusion.3), channel_id=2, replica_groups=mesh['grp'=16,'body'=32] {'grp'}, dimensions={0}, use_global_device_ids=true | all-gather | bytes 17408 | tf_op jit(solution)/shard_map/all_gather | solution.py:76
  316.6 111.6 %psum.23 = bf16[16,1024]{1,0:T(8,128)(2,1)S(1)} all-reduce(f32[16,1024]{1,0:T(8,128)S(1)} %pad_maximum_fusion.1), channel_id=1, replica_groups=mesh['grp'=16,'body'=32] {'body'}, use_global_device_ids=true, to_apply=%region_4.5 | all-reduce | flops 16384 | bytes 98304 | tf_op jit(solution)/shard_map/psum | solution.py:82
  428.9 1.4 maximum_add_fusion
  (99 shorter events, 20.5 us)
Async XLA Ops:
  6.5 46.2 %copy-start = (bf16[225,2,512]{2,1,0:T(2,128)(2,1)S(1)}, bf16[225,2,512]{2,1,0:T(2,128)(2,1)}, u32[]{:S(2)}) copy-start(bf16[225,2,512]{2,1,0:T(2,128)(2,1)} %param.14) | copy-start | bytes 1382404
  6.5 422.3 %all-reduce.2.cloned.1.call-start = ((), (), s32[]{:S(2)}) async-start(), calls=%async_computation | async-start | bytes 2097152 | tf_op jit(solution)/shard_map/psum | solution.py:65
  53.7 119.1 %copy-start.2 = (bf16[1,2,256,512]{3,2,1,0:T(8,128)(2,1)S(1)}, bf16[1,2,256,512]{3,2,1,0:T(8,128)(2,1)}, u32[]{:S(2)}) copy-start(bf16[1,2,256,512]{3,2,1,0:T(8,128)(2,1)} %param.17) | copy-start | bytes 1572868
  172.7 142.6 %copy-start.3 = (bf16[1,16,2,16,512]{4,3,2,1,0:T(8,128)(2,1)S(1)}, bf16[1,16,2,16,512]{4,3,2,1,0:T(8,128)(2,1)}, u32[]{:S(2)}) copy-start(bf16[1,16,2,16,512]{4,3,2,1,0:T(8,128)(2,1)} %param.19) | copy-start | bytes 1572868
  173.1 255.2 %copy-start.1 = (bf16[1,2,512,256]{3,2,1,0:T(8,128)(2,1)S(1)}, bf16[1,2,512,256]{3,2,1,0:T(8,128)(2,1)}, u32[]{:S(2)}) copy-start(bf16[1,2,512,256]{3,2,1,0:T(8,128)(2,1)} %param.18) | copy-start | bytes 1572868
  315.4 113.5 %copy-start.4 = (f32[1,16,512]{2,1,0:T(8,128)S(1)}, f32[1,16,512]{2,1,0:T(8,128)}, u32[]{:S(2)}) copy-start(f32[1,16,512]{2,1,0:T(8,128)} %param.12) | copy-start | bytes 98308
Sparse Core Ops, SparseCore 0:
  172.9 232.2 all-reduce.1
where the time goes:
time: 438 us; the launch traced here: 437 us
  blocking collectives  291 us (66%)
  local copies, waits for them, and re-layouts  110 us (25%)
  between operations  15.6 us (4%)
  matrix products  12.5 us (3%)
  other arithmetic  8.4 us (2%)
    psum x1, blocking collectives, local(): incoming = lax.psum(incoming_part, 'body').astype(jnp.bfloat16)  112 us
    psum x1, blocking collectives, local(): expansion = lax.psum(partial_value, 'body').astype(jnp.bfloat16)  102 us
    reshape x8, local copies, waits for them, and re-layouts, toeplitz_mats(): window.reshape(sequences.shape[:-1] + (length, 2 * length - 1))  48.7 us
    all_gather x1, blocking collectives, local(): piece = lax.all_gather(own_block, 'grp', axis=0, tiled=True)  39.8 us
    all_gather x1, blocking collectives, local(): all_offsets = lax.all_gather(offsets, 'body', axis=0, tiled=True)  37.1 us
    slice x8, local copies, waits for them, and re-layouts, toeplitz_mats(): window = tiled[..., length:length + length * (2 * length - 1)]  35.2 us
    another operation x24, local copies, waits for them, and re-layouts, toeplitz_mats(): tiled = jnp.tile(sequences, repeats)  23.8 us
  transfers between devices with their start and end apart: 1, of which 0 were waited for; matrix products, arithmetic and copies ran while one was open for 1% of the time, Pallas kernels for 0%

commit v1 on v0

v1 whole, which is shorter than its diff:
```python
import functools

import jax
import jax.numpy as jnp
from jax import lax
from jax.experimental import pallas as pl
from jax.experimental.pallas import tpu as pltpu
from jax.sharding import PartitionSpec as P

BF16 = jnp.bfloat16
F32 = jnp.float32
LANE = 128
ROWS = 16
GRP = 16
NY = 8
CELL = 4
MODES = 256
COEFS = 512


def dot(a, b):
    return jnp.dot(a, b, preferred_element_type=F32)


def paired(re, im):
    return jnp.concatenate(
        [jnp.concatenate([re, -im], axis=1), jnp.concatenate([im, re], axis=1)], axis=0
    )


def kernel(
    incident,
    exciting,
    t_maps,
    table,
    offsets,
    slots,
    up_maps,
    down_maps,
    group_maps,
    out,
    v_inc,
    v_exc,
    v_t,
    v_table,
    s_off,
    s_slot,
    v_up,
    v_down,
    v_gm,
    scat,
    near_out,
    near_in,
    u_out,
    u_in,
    e_out,
    e_in,
    g_out,
    g_in,
    p_out,
    p_in,
    q_out,
    q_in,
    i_all,
    load_sem,
    send_sem,
    recv_sem,
    near_send_sem,
):
    g = lax.axis_index("grp")
    b = lax.axis_index("body")
    y = b // CELL
    c = b % CELL

    loads = [
        pltpu.make_async_copy(src, dst, load_sem.at[k])
        for k, (src, dst) in enumerate(
            [
                (incident.at[0], v_inc),
                (t_maps.at[0], v_t),
                (offsets, s_off.at[pl.ds(0, 1)]),
                (slots, s_slot),
                (up_maps.at[0], v_up),
                (table, v_table),
                (group_maps.at[0], v_gm),
                (down_maps.at[0], v_down),
                (exciting.at[0], v_exc),
            ]
        )
    ]
    for copy in loads:
        copy.start()
    l_inc, l_t, l_off, l_slot, l_up, l_table, l_gm, l_down, l_exc = loads

    def y_peer(d):
        return {"grp": g, "body": lax.rem(y + d, NY) * CELL + c}

    def cell_peer(d):
        return {"grp": g, "body": y * CELL + lax.rem(c + d, CELL)}

    def grp_peer(d):
        return {"grp": lax.rem(g + d, GRP), "body": b}

    barrier = pltpu.get_barrier_semaphore()

    def greet(peer, count):
        def one(d, carry):
            pl.semaphore_signal(barrier, inc=1, device_id=peer(d), device_id_type=pl.DeviceIdType.MESH)
            return carry

        lax.fori_loop(1, count, one, 0)

    greet(cell_peer, CELL)
    greet(y_peer, NY)
    greet(grp_peer, GRP)

    def send(src, dst, phase, peer):
        return pltpu.make_async_remote_copy(
            src_ref=src,
            dst_ref=dst,
            send_sem=send_sem.at[phase],
            recv_sem=recv_sem.at[phase],
            device_id=peer,
            device_id_type=pl.DeviceIdType.MESH,
        )

    def send_all(count, make):
        def one(d, carry):
            make(d).start()
            return carry

        lax.fori_loop(1, count, one, 0)

    def wait_recv(ref, phase):
        pltpu.make_async_copy(ref, ref, recv_sem.at[phase]).wait()

    def wait_send(ref, phase):
        pltpu.make_async_copy(ref, ref, send_sem.at[phase]).wait()

    l_inc.wait()
    l_t.wait()
    x = v_inc[...]
    scattered = dot(
        paired(x[:, :MODES], x[:, MODES:]), v_t[...].reshape(2 * MODES, MODES)
    ).astype(BF16)
    scat[c] = scattered
    sr, si = scattered[:ROWS], scattered[ROWS:]
    own_pair = paired(sr, si)

    l_off.wait()
    pl.semaphore_wait(barrier, NY + CELL + GRP - 3)

    def send_off(d):
        return send(s_off.at[pl.ds(0, 1)], s_off.at[pl.ds(NY - d, 1)], 0, y_peer(d))

    def send_scat(d):
        return send(scat.at[c], scat.at[c], 1, cell_peer(d))

    send_all(NY, send_off)
    send_all(CELL, send_scat)

    l_up.wait()
    term = dot(own_pair, v_up[...].reshape(2 * MODES, COEFS)).astype(BF16)
    for t in range(4):
        u_out[t] = term[:, t * LANE : (t + 1) * LANE]

    def send_u(d):
        return send(u_out.at[lax.rem(y + d, NY) // 2], u_in.at[d - 1], 2, y_peer(d))

    send_all(NY, send_u)

    l_slot.wait()
    l_table.wait()
    wait_recv(scat.at[pl.ds(0, CELL - 1)], 1)
    wait_recv(s_off.at[pl.ds(0, NY - 1)], 0)
    lane = lax.broadcasted_iota(jnp.int32, (LANE, LANE), 1)
    sub = lax.broadcasted_iota(jnp.int32, (LANE, LANE), 0)
    wrapped = lane < sub

    def toeplitz(row):
        turned = [
            pltpu.roll(
                jnp.broadcast_to(row[:, k * LANE : (k + 1) * LANE], (LANE, LANE)),
                0,
                1,
                stride=1,
                stride_axis=0,
            )
            for k in range(4)
        ]
        wide = [
            jnp.where(wrapped, turned[k], turned[k + 1]).astype(BF16) for k in range(3)
        ]
        return jnp.concatenate(
            [
                jnp.concatenate([wide[1], wide[2]], axis=1),
                jnp.concatenate([wide[0], wide[1]], axis=1),
            ],
            axis=0,
        )

    def near_one(d):
        total = jnp.zeros((2 * ROWS, MODES), F32)
        for k in range(CELL):
            seq = v_table[s_off[d, s_slot[y * CELL + k]]].astype(F32)
            keep = jnp.logical_or(d != 0, k != c)
            seq = jnp.where(keep, seq, 0.0)
            mats = jnp.concatenate([toeplitz(seq[0:1]), toeplitz(seq[1:2])], axis=0)
            source = scat[k]
            total += dot(paired(source[:ROWS], source[ROWS:]), mats)
        return total

    def near_send(d):
        return pltpu.make_async_remote_copy(
            src_ref=near_out.at[d],
            dst_ref=near_in.at[d - 1],
            send_sem=near_send_sem,
            recv_sem=recv_sem.at[8],
            device_id=y_peer(d),
            device_id_type=pl.DeviceIdType.MESH,
        )

    def near_chunk(low, high):
        def one(d, carry):
            near_out[d] = near_one(d).astype(BF16)
            near_send(d).start()
            return carry

        lax.fori_loop(low, high, one, 0)

    near_chunk(1, 2)

    wait_recv(u_in, 2)
    e_sum = u_out[y // 2].astype(F32)
    for k in range(NY - 1):
        e_sum += u_in[k].astype(F32)
    e_out[...] = e_sum.astype(e_out.dtype)

    def send_e(d):
        return send(e_out, e_in.at[d - 1], 3, cell_peer(d))

    send_all(CELL, send_e)

    near_chunk(2, 3)

    wait_recv(e_in, 3)
    for k in range(CELL - 1):
        e_sum += e_in[k].astype(F32)
    own_block = lax.rem(b, 8)
    re_to = lax.rem(g, 8)
    im_to = lax.rem(g + 4, 8)
    re_part = pltpu.roll(e_sum[:ROWS], lax.rem(re_to - own_block + 8, 8) * 16, 1)
    im_part = pltpu.roll(e_sum[ROWS:], lax.rem(im_to - own_block + 8, 8) * 16, 1)
    block = lax.broadcasted_iota(jnp.int32, (ROWS, LANE), 1) // 16
    g_out[...] = jnp.where(block == re_to, re_part, im_part).astype(BF16)

    def send_g(d):
        return send(g_out, g_in.at[g], 4, grp_peer(d))

    send_all(GRP, send_g)
    g_in[g] = jnp.zeros((ROWS, LANE), BF16)

    near_chunk(3, 5)

    l_gm.wait()
    wait_recv(g_in.at[pl.ds(0, GRP - 1)], 4)
    res, ims = [], []
    for half in range(2):
        re = g_in[8 * half].astype(F32)
        im = re
        for k in range(1, 8):
            here = g_in[8 * half + k].astype(F32)
            re = jnp.where(block == k, here, re)
            im = jnp.where(block == (k + 4) % 8, here, im)
        res.append(re.astype(BF16))
        ims.append(pltpu.roll(im, 64, 1).astype(BF16))
    pair = paired(jnp.concatenate(res, axis=1), jnp.concatenate(ims, axis=1))
    gm = v_gm[...]
    mats = jnp.concatenate(
        [gm[:, 0].reshape(GRP * 16, COEFS), gm[:, 1].reshape(GRP * 16, COEFS)], axis=0
    )
    part = dot(pair, mats)
    for t in range(4):
        p_out[t] = part[:ROWS, t * LANE : (t + 1) * LANE].astype(BF16)
        p_out[4 + t] = part[ROWS:, t * LANE : (t + 1) * LANE].astype(BF16)

    def send_p(d):
        return send(p_out.at[lax.rem(y + d, NY)], p_in.at[d - 1], 5, y_peer(d))

    send_all(NY, send_p)

    near_chunk(5, 7)

    wait_recv(p_in, 5)
    q_sum = p_out[y].astype(F32)
    for k in range(NY - 1):
        q_sum += p_in[k].astype(F32)
    q_out[...] = q_sum.astype(q_out.dtype)

    def send_q(d):
        return send(q_out, q_in.at[d - 1], 6, cell_peer(d))

    send_all(CELL, send_q)

    near_chunk(7, 8)

    wait_recv(q_in, 6)
    for k in range(CELL - 1):
        q_sum += q_in[k].astype(F32)
    i_all[y] = q_sum.astype(BF16)

    def send_i(d):
        return send(i_all.at[y], i_all.at[y], 7, y_peer(d))

    send_all(NY, send_i)

    l_exc.wait()
    near = near_one(0)
    wait_recv(near_in, 8)
    for k in range(NY - 1):
        near += near_in[k].astype(F32)

    l_down.wait()
    wait_recv(i_all.at[pl.ds(0, NY - 1)], 7)
    incoming_re = jnp.concatenate([i_all[k] for k in range(4)], axis=1)
    incoming_im = jnp.concatenate([i_all[4 + k] for k in range(4)], axis=1)
    far = dot(paired(incoming_re, incoming_im), v_down[...].reshape(2 * COEFS, MODES))
    both = near + far
    out[0, :, :MODES] = v_exc[:, :MODES] + both[:ROWS]
    out[0, :, MODES:] = v_exc[:, MODES:] + both[ROWS:]

    wait_send(s_off.at[pl.ds(0, NY - 1)], 0)
    wait_send(scat.at[pl.ds(0, CELL - 1)], 1)
    wait_send(u_in, 2)
    wait_send(e_in, 3)
    wait_send(g_in.at[pl.ds(0, GRP - 1)], 4)
    wait_send(p_in, 5)
    wait_send(q_in, 6)
    wait_send(i_all.at[pl.ds(0, NY - 1)], 7)
    pltpu.make_async_copy(near_in, near_in, near_send_sem).wait()


def local(*args):
    anywhere = pl.BlockSpec(memory_space=pl.ANY)
    vmem = pltpu.VMEM
    return pl.pallas_call(
        kernel,
        out_shape=jax.ShapeDtypeStruct((1, ROWS, 2 * MODES), F32),
        in_specs=[anywhere] * 9,
        out_specs=pl.BlockSpec(memory_space=pltpu.VMEM),
        scratch_shapes=[
            vmem((ROWS, 2 * MODES), BF16),
            vmem((ROWS, 2 * MODES), F32),
            vmem((2, MODES, MODES), BF16),
            vmem((225, 2, 512), BF16),
            pltpu.SMEM((NY, 32), jnp.int32),
            pltpu.SMEM((32,), jnp.int32),
            vmem((2, MODES, COEFS), BF16),
            vmem((2, COEFS, MODES), BF16),
            vmem((GRP, 2, 16, COEFS), BF16),
            vmem((CELL, 2 * ROWS, MODES), BF16),
            vmem((NY, 2 * ROWS, MODES), BF16),
            vmem((NY - 1, 2 * ROWS, MODES), BF16),
            vmem((4, 2 * ROWS, LANE), BF16),
            vmem((NY - 1, 2 * ROWS, LANE), BF16),
            vmem((2 * ROWS, LANE), BF16),
            vmem((CELL - 1, 2 * ROWS, LANE), BF16),
            vmem((ROWS, LANE), BF16),
            vmem((GRP, ROWS, LANE), BF16),
            vmem((NY, ROWS, LANE), BF16),
            vmem((NY - 1, ROWS, LANE), BF16),
            vmem((ROWS, LANE), BF16),
            vmem((CELL - 1, ROWS, LANE), BF16),
            vmem((NY, ROWS, LANE), BF16),
            pltpu.SemaphoreType.DMA((9,)),
            pltpu.SemaphoreType.DMA((8,)),
            pltpu.SemaphoreType.DMA((9,)),
            pltpu.SemaphoreType.DMA,
        ],
        compiler_params=pltpu.CompilerParams(
            collective_id=0, has_side_effects=True, vmem_limit_bytes=32 * 1024 * 1024
        ),
        name="scatter_step",
    )(*args)


def solution(mesh):
    return jax.shard_map(
        local,
        mesh=mesh,
        in_specs=(
            P(("grp", "body"), None, None),
            P(("grp", "body"), None, None),
            P(("grp", "body"), None, None, None),
            P(),
            P(("grp", "body"), None),
            P("grp"),
            P(("grp", "body"), None, None, None),
            P(("grp", "body"), None, None, None),
            P("grp", None, None, "body", None),
        ),
        out_specs=P(("grp", "body"), None, None),
        check_vma=False,
    )
```

time: 438 us -> 51.2 us (0.12)
  blocking collectives: 291 us -> 0 us
  local copies, waits for them, and re-layouts: 110 us -> 8.49 us
  Pallas kernels: 0 us -> 42.2 us
  between operations: 15.6 us -> 0.02 us
  matrix products: 12.5 us -> 0 us
  other arithmetic: 8.4 us -> 0 us
    psum x2 -> x0, blocking collectives: 214 us -> none  [the longest x1 112 us: local(): incoming = lax.psum(incoming_part, 'body').astype(jnp.bfloat16)]
    all_gather x2 -> x0, blocking collectives: 76.8 us -> none  [the longest x1 39.8 us: local(): piece = lax.all_gather(own_block, 'grp', axis=0, tiled=True)]
    reshape x8 -> x0, local copies, waits for them, and re-layouts: 48.7 us -> none  [toeplitz_mats(): window.reshape(sequences.shape[:-1] + (length, 2 * length - 1))]
    pallas_call x0 -> x1, Pallas kernels: none -> 42.2 us  [local(): pl.pallas_call(kernel, out_shape=jax.ShapeDtypeStruct((1, ROWS, 2 * MODES...]
    slice x8 -> x0, local copies, waits for them, and re-layouts: 35.2 us -> none  [toeplitz_mats(): window = tiled[..., length:length + length * (2 * length - 1)]]
    another operation x24 -> x0, local copies, waits for them, and re-layouts: 23.8 us -> none  [toeplitz_mats(): tiled = jnp.tile(sequences, repeats)]
    dot_general x48 -> x0, matrix products: 12.5 us -> none  [the longest x12 3.2 us: complex_apply(): jnp.einsum(form, imag_values, real_mats, preferred_element_type=jnp.float32)]
    unnamed x11 -> x19, local copies, waits for them, and re-layouts: 0.06 us -> 8.49 us
  transfers between devices with their start and end apart: 1 -> 0, of which waited for: 0 -> 0; matrix products, arithmetic and copies ran while one was open for 1% -> 0% of each run, Pallas kernels for 0% -> 0%
where the time goes in v1:
time: 51.2 us; the launch traced here: 50.7 us
  Pallas kernels  42.2 us (82%)
  local copies, waits for them, and re-layouts  8.49 us (17%)
    pallas_call x1, Pallas kernels, local(): pl.pallas_call(kernel, out_shape=jax.ShapeDtypeStruct((1, ROWS, 2 * MODES...  42.2 us
    unnamed x19, local copies, waits for them, and re-layouts  8.49 us

profile of v1, /device:TPU:1, one launch (start us, length us, event | category | flops | bytes accessed | tf_op | source)
XLA Modules:
  0.0 50.7 jit_solution(5352819875327439939)
XLA Ops:
  0.0 0.0 copy-start
  0.0 1.0 %copy-done = bf16[1,2,256,512]{3,2,1,0:T(8,128)(2,1)S(1)} copy-done((bf16[1,2,256,512]{3,2,1,0:T(8,128)(2,1)S(1)}, bf16[1,2,256,512]{3,2,1,0:T(8,128)(2,1)}, u32[]{:S(2)}) %copy-start) | copy-done | bytes 524312
  1.0 0.0 copy-start.1
  1.0 1.0 %copy-done.1 = bf16[1,2,512,256]{3,2,1,0:T(8,128)(2,1)S(1)} copy-done((bf16[1,2,512,256]{3,2,1,0:T(8,128)(2,1)S(1)}, bf16[1,2,512,256]{3,2,1,0:T(8,128)(2,1)}, u32[]{:S(2)}) %copy-start.1) | copy-done | bytes 524312
  2.1 0.0 copy-start.2
  2.1 1.0 %copy-done.2 = bf16[1,16,2,16,512]{4,3,2,1,0:T(8,128)(2,1)S(1)} copy-done((bf16[1,16,2,16,512]{4,3,2,1,0:T(8,128)(2,1)S(1)}, bf16[1,16,2,16,512]{4,3,2,1,0:T(8,128)(2,1)}, u32[]{:S(2)}) %copy-start.2) | copy-done | bytes 524312
  3.1 0.0 copy-start.3
  3.1 1.0 %copy-done.3 = bf16[225,2,512]{2,1,0:T(2,128)(2,1)S(1)} copy-done((bf16[225,2,512]{2,1,0:T(2,128)(2,1)S(1)}, bf16[225,2,512]{2,1,0:T(2,128)(2,1)}, u32[]{:S(2)}) %copy-start.3) | copy-done | bytes 460824
  4.1 0.0 copy-start.4
  4.1 0.9 %copy-done.4 = bf16[1,2,256,256]{3,2,1,0:T(8,128)(2,1)S(1)} copy-done((bf16[1,2,256,256]{3,2,1,0:T(8,128)(2,1)S(1)}, bf16[1,2,256,256]{3,2,1,0:T(8,128)(2,1)}, u32[]{:S(2)}) %copy-start.4) | copy-done | bytes 262168
  5.1 0.0 copy-start.5
  5.1 0.8 %copy-done.5 = f32[1,16,512]{2,1,0:T(8,128)S(1)} copy-done((f32[1,16,512]{2,1,0:T(8,128)S(1)}, f32[1,16,512]{2,1,0:T(8,128)}, u32[]{:S(2)}) %copy-start.5) | copy-done | bytes 32792
  5.9 0.0 copy-start.6
  5.9 0.7 %copy-done.6 = bf16[1,16,512]{2,1,0:T(8,128)(2,1)S(1)} copy-done((bf16[1,16,512]{2,1,0:T(8,128)(2,1)S(1)}, bf16[1,16,512]{2,1,0:T(8,128)(2,1)}, u32[]{:S(2)}) %copy-start.6) | copy-done | bytes 16408
  6.6 0.0 copy-start.7
  6.6 0.7 %copy-done.7 = s32[1,32]{1,0:T(1,128)S(1)} copy-done((s32[1,32]{1,0:T(1,128)S(1)}, s32[1,32]{1,0:T(1,128)}, u32[]{:S(2)}) %copy-start.7) | copy-done | bytes 152
  7.2 0.0 copy-start.8
  7.2 0.7 %copy-done.8 = s32[32]{0:T(128)S(1)} copy-done((s32[32]{0:T(128)S(1)}, s32[32]{0:T(128)}, u32[]{:S(2)}) %copy-start.8) | copy-done | bytes 152
  7.9 42.2 %scatter_step.1 = f32[1,16,512]{2,1,0:T(8,128)S(1)} custom-call(bf16[1,16,512]{2,1,0:T(8,128)(2,1)S(1)} %copy-done.6, f32[1,16,512]{2,1,0:T(8,128)S(1)} %copy-done.5, bf16[1,2,256,256]{3,2,1,0:T(8,128)(2,1)S(1)} %copy-done.4, bf16[225,2,512]{2,1,0:T(2,128)(2,1)S(1)} %copy-done.3, s32[1,32]{1,0:T(1,128)S(1)} %copy-done.7, s32[32]{0:T(128)S(1)} %copy-done.8, ...), custom_call_target="tpu_custom_call" | custom-call | tf_op jit(solution)/shard_map/scatter_step/pallas_call | solution.py:346
  50.1 0.6 %copy.11 = f32[1,16,512]{2,1,0:T(8,128)} copy(f32[1,16,512]{2,1,0:T(8,128)S(1)} %scatter_step.1) | data formatting | bytes 65536
Async XLA Ops:
  0.0 1.0 %copy-start = (bf16[1,2,256,512]{3,2,1,0:T(8,128)(2,1)S(1)}, bf16[1,2,256,512]{3,2,1,0:T(8,128)(2,1)}, u32[]{:S(2)}) copy-start(bf16[1,2,256,512]{3,2,1,0:T(8,128)(2,1)} %up_maps.1) | copy-start | bytes 1572868
  1.0 1.0 %copy-start.1 = (bf16[1,2,512,256]{3,2,1,0:T(8,128)(2,1)S(1)}, bf16[1,2,512,256]{3,2,1,0:T(8,128)(2,1)}, u32[]{:S(2)}) copy-start(bf16[1,2,512,256]{3,2,1,0:T(8,128)(2,1)} %down_maps.1) | copy-start | bytes 1572868
  2.1 1.0 %copy-start.2 = (bf16[1,16,2,16,512]{4,3,2,1,0:T(8,128)(2,1)S(1)}, bf16[1,16,2,16,512]{4,3,2,1,0:T(8,128)(2,1)}, u32[]{:S(2)}) copy-start(bf16[1,16,2,16,512]{4,3,2,1,0:T(8,128)(2,1)} %group_maps.1) | copy-start | bytes 1572868
  3.1 1.0 %copy-start.3 = (bf16[225,2,512]{2,1,0:T(2,128)(2,1)S(1)}, bf16[225,2,512]{2,1,0:T(2,128)(2,1)}, u32[]{:S(2)}) copy-start(bf16[225,2,512]{2,1,0:T(2,128)(2,1)} %table.1) | copy-start | bytes 1382404
  4.1 0.9 %copy-start.4 = (bf16[1,2,256,256]{3,2,1,0:T(8,128)(2,1)S(1)}, bf16[1,2,256,256]{3,2,1,0:T(8,128)(2,1)}, u32[]{:S(2)}) copy-start(bf16[1,2,256,256]{3,2,1,0:T(8,128)(2,1)} %t_maps.1) | copy-start | bytes 786436
  5.1 0.8 %copy-start.5 = (f32[1,16,512]{2,1,0:T(8,128)S(1)}, f32[1,16,512]{2,1,0:T(8,128)}, u32[]{:S(2)}) copy-start(f32[1,16,512]{2,1,0:T(8,128)} %exciting.1) | copy-start | bytes 98308
  5.9 0.7 %copy-start.6 = (bf16[1,16,512]{2,1,0:T(8,128)(2,1)S(1)}, bf16[1,16,512]{2,1,0:T(8,128)(2,1)}, u32[]{:S(2)}) copy-start(bf16[1,16,512]{2,1,0:T(8,128)(2,1)} %incident.1) | copy-start | bytes 49156
  6.6 0.7 %copy-start.7 = (s32[1,32]{1,0:T(1,128)S(1)}, s32[1,32]{1,0:T(1,128)}, u32[]{:S(2)}) copy-start(s32[1,32]{1,0:T(1,128)} %offsets.1) | copy-start | bytes 388
  7.2 0.7 %copy-start.8 = (s32[32]{0:T(128)S(1)}, s32[32]{0:T(128)}, u32[]{:S(2)}) copy-start(s32[32]{0:T(128)} %slots.1) | copy-start | bytes 388

commit v2 on v1

--- a/solution.py
+++ b/solution.py
@@ -234,7 +234,7 @@
     e_sum = u_out[y // 2].astype(F32)
     for k in range(NY - 1):
         e_sum += u_in[k].astype(F32)
-    e_out[...] = e_sum.astype(e_out.dtype)
+    e_out[...] = e_sum
 
     def send_e(d):
         return send(e_out, e_in.at[d - 1], 3, cell_peer(d))
@@ -245,7 +245,7 @@
 
     wait_recv(e_in, 3)
     for k in range(CELL - 1):
-        e_sum += e_in[k].astype(F32)
+        e_sum += e_in[k]
     own_block = lax.rem(b, 8)
     re_to = lax.rem(g, 8)
     im_to = lax.rem(g + 4, 8)
@@ -281,8 +281,8 @@
     )
     part = dot(pair, mats)
     for t in range(4):
-        p_out[t] = part[:ROWS, t * LANE : (t + 1) * LANE].astype(BF16)
-        p_out[4 + t] = part[ROWS:, t * LANE : (t + 1) * LANE].astype(BF16)
+        p_out[t] = part[:ROWS, t * LANE : (t + 1) * LANE]
+        p_out[4 + t] = part[ROWS:, t * LANE : (t + 1) * LANE]
 
     def send_p(d):
         return send(p_out.at[lax.rem(y + d, NY)], p_in.at[d - 1], 5, y_peer(d))
@@ -292,10 +292,10 @@
     near_chunk(5, 7)
 
     wait_recv(p_in, 5)
-    q_sum = p_out[y].astype(F32)
+    q_sum = p_out[y]
     for k in range(NY - 1):
-        q_sum += p_in[k].astype(F32)
-    q_out[...] = q_sum.astype(q_out.dtype)
+        q_sum += p_in[k]
+    q_out[...] = q_sum
 
     def send_q(d):
         return send(q_out, q_in.at[d - 1], 6, cell_peer(d))
@@ -306,7 +306,7 @@
 
     wait_recv(q_in, 6)
     for k in range(CELL - 1):
-        q_sum += q_in[k].astype(F32)
+        q_sum += q_in[k]
     i_all[y] = q_sum.astype(BF16)
 
     def send_i(d):
@@ -363,14 +363,14 @@
             vmem((NY - 1, 2 * ROWS, MODES), BF16),
             vmem((4, 2 * ROWS, LANE), BF16),
             vmem((NY - 1, 2 * ROWS, LANE), BF16),
-            vmem((2 * ROWS, LANE), BF16),
-            vmem((CELL - 1, 2 * ROWS, LANE), BF16),
+            vmem((2 * ROWS, LANE), F32),
+            vmem((CELL - 1, 2 * ROWS, LANE), F32),
             vmem((ROWS, LANE), BF16),
             vmem((GRP, ROWS, LANE), BF16),
-            vmem((NY, ROWS, LANE), BF16),
-            vmem((NY - 1, ROWS, LANE), BF16),
-            vmem((ROWS, LANE), BF16),
-            vmem((CELL - 1, ROWS, LANE), BF16),
+            vmem((NY, ROWS, LANE), F32),
+            vmem((NY - 1, ROWS, LANE), F32),
+            vmem((ROWS, LANE), F32),
+            vmem((CELL - 1, ROWS, LANE), F32),
             vmem((NY, ROWS, LANE), BF16),
             pltpu.SemaphoreType.DMA((9,)),
             pltpu.SemaphoreType.DMA((8,)),
@@ -378,7 +378,7 @@
             pltpu.SemaphoreType.DMA,
         ],
         compiler_params=pltpu.CompilerParams(
-            collective_id=0, has_side_effects=True, vmem_limit_bytes=32 * 1024 * 1024
+            collective_id=0, has_side_effects=True, vmem_limit_bytes=63 * 1024 * 1024
         ),
         name="scatter_step",
     )(*args)

time: 51.2 us -> 44.7 us (0.87)
  local copies, waits for them, and re-layouts: 8.49 us -> 1.38 us
  Pallas kernels: 42.2 us -> 43.1 us
    unnamed x19 -> x1, local copies, waits for them, and re-layouts: 8.49 us -> 1.38 us
    pallas_call x1, Pallas kernels: 42.2 us -> 43.1 us  [local(): pl.pallas_call(kernel, out_shape=jax.ShapeDtypeStruct((1, ROWS, 2 * MODES...]
where the time goes in v2:
time: 44.7 us; the launch traced here: 44.5 us
  Pallas kernels  43.1 us (96%)
  local copies, waits for them, and re-layouts  1.38 us (3%)
    pallas_call x1, Pallas kernels, local(): pl.pallas_call(kernel, out_shape=jax.ShapeDtypeStruct((1, ROWS, 2 * MODES...  43.1 us
    unnamed x1, local copies, waits for them, and re-layouts  1.38 us

profile of v2, /device:TPU:1, one launch (start us, length us, event | category | flops | bytes accessed | tf_op | source)
XLA Modules:
  0.0 44.5 jit_solution(7344501780892451661)
XLA Ops:
  0.0 43.1 %scatter_step.1 = f32[1,16,512]{2,1,0:T(8,128)} custom-call(bf16[1,16,512]{2,1,0:T(8,128)(2,1)} %incident.1, f32[1,16,512]{2,1,0:T(8,128)} %exciting.1, bf16[1,2,256,256]{3,2,1,0:T(8,128)(2,1)} %t_maps.1, bf16[225,2,512]{2,1,0:T(2,128)(2,1)} %table.1, s32[1,32]{1,0:T(1,128)} %offsets.1, s32[32]{0:T(128)} %slots.1, bf16[1,2,256,512]{3,2,1,0:T(8,128)(2,1)} %up_maps.1, ...), custom_call_target="tpu_custom_call" | custom-call | tf_op jit(solution)/shard_map/scatter_step/pallas_call | solution.py:346
  43.1 1.4 %copy.11 = f32[1,16,512]{2,1,0:T(8,128)} copy(f32[1,16,512]{2,1,0:T(8,128)} %scatter_step.1) | data formatting | bytes 65536

commit v3 on v2

v3 whole, which is shorter than its diff:
```python
import functools

import jax
import jax.numpy as jnp
from jax import lax
from jax.experimental import pallas as pl
from jax.experimental.pallas import tpu as pltpu
from jax.sharding import PartitionSpec as P

BF16 = jnp.bfloat16
F32 = jnp.float32
LANE = 128
ROWS = 16
HALF = 64
GRP = 16
NY = 8
CELL = 4
MODES = 256
COEFS = 512


def dot(a, b):
    return jnp.dot(a, b, preferred_element_type=F32)


def paired(re, im):
    return jnp.concatenate(
        [jnp.concatenate([re, -im], axis=1), jnp.concatenate([im, re], axis=1)], axis=0
    )


BODY_STEPS = [
    (dy, dc)
    for dy in (4, 3, 5, 2, 6, 1, 7, 0)
    for dc in (2, 3, 1, 0)
    if (dy, dc) != (0, 0)
]
Y_STEPS = (4, 3, 5, 2, 6, 1, 7)
CELL_STEPS = (2, 3, 1)
GRP_STEPS = sorted(
    [(dx, dz) for dx in range(4) for dz in range(4) if (dx, dz) != (0, 0)],
    key=lambda s: -(min(s[0], 4 - s[0]) + 2 * min(s[1], 4 - s[1])),
)


def kernel(
    incident,
    exciting,
    t_maps,
    table,
    offsets,
    slots,
    up_maps,
    down_maps,
    group_maps,
    out,
    v_inc,
    v_exc,
    v_t,
    v_table,
    s_off,
    s_slot,
    v_up,
    v_down,
    w_gm,
    scat,
    near_out,
    near_in,
    u_out,
    u_in,
    g_out,
    g_in,
    p_out,
    p_in,
    i_all,
    load_sem,
    send_sem,
    recv_sem,
):
    g = lax.axis_index("grp")
    b = lax.axis_index("body")
    y = b // CELL
    c = b % CELL
    gx = g // 4
    gz = g % 4

    def quarter(member):
        return group_maps.at[0, :, :, :, pl.ds(pl.multiple_of(member * LANE, LANE), LANE)]

    loads = [
        pltpu.make_async_copy(src, dst, load_sem.at[k])
        for k, (src, dst) in enumerate(
            [
                (incident.at[0], v_inc),
                (t_maps.at[0], v_t),
                (up_maps.at[0], v_up),
                (offsets, s_off.at[pl.ds(0, 1)]),
                (slots, s_slot),
                (table, v_table),
                (quarter(c), w_gm.at[:, :, c]),
                (down_maps.at[0], v_down),
                (exciting.at[0], v_exc),
            ]
        )
    ]
    for copy in loads:
        copy.start()
    l_inc, l_t, l_up, l_off, l_slot, l_table, l_gm, l_down, l_exc = loads

    def body_peer(step):
        dy, dc = step
        return {"grp": g, "body": lax.rem(y + dy, NY) * CELL + lax.rem(c + dc, CELL)}

    def y_peer(d):
        return body_peer((d, 0))

    def cell_peer(d):
        return body_peer((0, d))

    def grp_peer(step):
        dx, dz = step
        return {"grp": lax.rem(gx + dx, 4) * 4 + lax.rem(gz + dz, 4), "body": b}

    barrier = pltpu.get_barrier_semaphore()
    for peer in [grp_peer(s) for s in GRP_STEPS] + [body_peer(s) for s in BODY_STEPS]:
        pl.semaphore_signal(barrier, inc=1, device_id=peer, device_id_type=pl.DeviceIdType.MESH)

    def send(src, dst, phase, peer):
        pltpu.make_async_remote_copy(
            src_ref=src,
            dst_ref=dst,
            send_sem=send_sem.at[phase],
            recv_sem=recv_sem.at[phase],
            device_id=peer,
            device_id_type=pl.DeviceIdType.MESH,
        ).start()

    def wait_recv(ref, phase):
        pltpu.make_async_copy(ref, ref, recv_sem.at[phase]).wait()

    def wait_send(ref, phase):
        pltpu.make_async_copy(ref, ref, send_sem.at[phase]).wait()

    l_inc.wait()
    l_t.wait()
    x = v_inc[...]
    scattered = dot(
        paired(x[:, :MODES], x[:, MODES:]), v_t[...].reshape(2 * MODES, MODES)
    ).astype(BF16)
    scat[c] = scattered
    own_pair = paired(scattered[:ROWS], scattered[ROWS:])

    l_up.wait()
    term = dot(own_pair, v_up[...].reshape(2 * MODES, COEFS))
    low = lax.broadcasted_iota(jnp.int32, (ROWS, LANE), 1) < HALF
    for t in range(4):
        re = term[:ROWS, t * LANE : (t + 1) * LANE]
        im = term[ROWS:, t * LANE : (t + 1) * LANE]
        u_out[2 * t] = jnp.where(low, re, pltpu.roll(im, HALF, 1)).astype(BF16)
        u_out[2 * t + 1] = jnp.where(low, pltpu.roll(re, HALF, 1), im).astype(BF16)
    l_off.wait()

    pl.semaphore_wait(barrier, len(BODY_STEPS) + len(GRP_STEPS))
    for k, step in enumerate(BODY_STEPS):
        send(u_out.at[lax.rem(y + step[0], NY)], u_in.at[k], 2, body_peer(step))
    for d in Y_STEPS:
        send(s_off.at[pl.ds(0, 1)], s_off.at[pl.ds(NY - d, 1)], 0, y_peer(d))
    for d in CELL_STEPS:
        send(scat.at[c], scat.at[c], 1, cell_peer(d))
    for d in CELL_STEPS:
        send(quarter(lax.rem(c + d, CELL)), w_gm.at[:, :, c], 3, cell_peer(d))

    wait_recv(u_in, 2)
    e_sum = u_out[y].astype(F32)
    for k in range(len(BODY_STEPS)):
        e_sum += u_in[k].astype(F32)
    g_out[...] = e_sum.astype(BF16)
    for step in GRP_STEPS:
        send(g_out, g_in.at[g], 4, grp_peer(step))
    g_in[g] = jnp.zeros((ROWS, LANE), BF16)

    l_slot.wait()
    l_table.wait()
    wait_recv(scat.at[pl.ds(0, CELL - 1)], 1)
    wait_recv(s_off.at[pl.ds(0, NY - 1)], 0)
    lane = lax.broadcasted_iota(jnp.int32, (LANE, LANE), 1)
    sub = lax.broadcasted_iota(jnp.int32, (LANE, LANE), 0)
    wrapped = lane < sub

    def toeplitz(row):
        turned = [
            pltpu.roll(
                jnp.broadcast_to(row[:, k * LANE : (k + 1) * LANE], (LANE, LANE)),
                0,
                1,
                stride=1,
                stride_axis=0,
            )
            for k in range(4)
        ]
        wide = [
            jnp.where(wrapped, turned[k], turned[k + 1]).astype(BF16) for k in range(3)
        ]
        return jnp.concatenate(
            [
                jnp.concatenate([wide[1], wide[2]], axis=1),
                jnp.concatenate([wide[0], wide[1]], axis=1),
            ],
            axis=0,
        )

    def near_one(d):
        total = jnp.zeros((2 * ROWS, MODES), F32)
        for k in range(CELL):
            seq = v_table[s_off[d, s_slot[y * CELL + k]]].astype(F32)
            keep = jnp.logical_or(d != 0, k != c)
            seq = jnp.where(keep, seq, 0.0)
            mats = jnp.concatenate([toeplitz(seq[0:1]), toeplitz(seq[1:2])], axis=0)
            source = scat[k]
            total += dot(paired(source[:ROWS], source[ROWS:]), mats)
        return total

    def near_chunk(low, high):
        def one(d, carry):
            near_out[d] = near_one(d).astype(BF16)
            send(near_out.at[d], near_in.at[d - 1], 6, y_peer(d))
            return carry

        lax.fori_loop(low, high, one, 0)

    near_chunk(1, NY)

    l_gm.wait()
    wait_recv(w_gm.at[:, :, pl.ds(0, CELL - 1)], 3)
    wait_recv(g_in.at[pl.ds(0, GRP - 1)], 4)
    tops, bottoms = [], []
    for h in range(GRP):
        pair = g_in[h].astype(F32)
        tops.append(jnp.where(low, pair, -pair).astype(BF16))
        bottoms.append(pltpu.roll(pair, HALF, 1).astype(BF16))
    left = jnp.concatenate(
        [jnp.concatenate(tops, axis=1), jnp.concatenate(bottoms, axis=1)], axis=0
    )
    p_sum = dot(left, w_gm[...].reshape(GRP * LANE, LANE))
    p_out[...] = p_sum.astype(BF16)
    for k, d in enumerate(Y_STEPS):
        send(p_out, p_in.at[k], 5, y_peer(d))

    near = near_one(0)
    wait_recv(p_in, 5)
    for k in range(NY - 1):
        p_sum += p_in[k].astype(F32)
    i_all[c] = p_sum.astype(BF16)
    for d in CELL_STEPS:
        send(i_all.at[c], i_all.at[c], 7, cell_peer(d))

    wait_recv(near_in, 6)
    for k in range(NY - 1):
        near += near_in[k].astype(F32)
    l_exc.wait()
    near_re = v_exc[:, :MODES] + near[:ROWS]
    near_im = v_exc[:, MODES:] + near[ROWS:]

    l_down.wait()
    wait_recv(i_all.at[pl.ds(0, CELL - 1)], 7)
    incoming_re = jnp.concatenate([i_all[k][:ROWS] for k in range(CELL)], axis=1)
    incoming_im = jnp.concatenate([i_all[k][ROWS:] for k in range(CELL)], axis=1)
    far = dot(paired(incoming_re, incoming_im), v_down[...].reshape(2 * COEFS, MODES))
    out[0, :, :MODES] = near_re + far[:ROWS]
    out[0, :, MODES:] = near_im + far[ROWS:]

    wait_send(s_off.at[pl.ds(0, NY - 1)], 0)
    wait_send(scat.at[pl.ds(0, CELL - 1)], 1)
    wait_send(u_in, 2)
    wait_send(w_gm.at[:, :, pl.ds(0, CELL - 1)], 3)
    wait_send(g_in.at[pl.ds(0, GRP - 1)], 4)
    wait_send(p_in, 5)
    wait_send(near_in, 6)
    wait_send(i_all.at[pl.ds(0, CELL - 1)], 7)


def local(*args):
    anywhere = pl.BlockSpec(memory_space=pl.ANY)
    vmem = pltpu.VMEM
    return pl.pallas_call(
        kernel,
        out_shape=jax.ShapeDtypeStruct((1, ROWS, 2 * MODES), F32),
        in_specs=[anywhere] * 9,
        out_specs=pl.BlockSpec(memory_space=pltpu.VMEM),
        scratch_shapes=[
            vmem((ROWS, 2 * MODES), BF16),
            vmem((ROWS, 2 * MODES), F32),
            vmem((2, MODES, MODES), BF16),
            vmem((225, 2, 512), BF16),
            pltpu.SMEM((NY, 32), jnp.int32),
            pltpu.SMEM((32,), jnp.int32),
            vmem((2, MODES, COEFS), BF16),
            vmem((2, COEFS, MODES), BF16),
            vmem((GRP, 2, CELL, 16, LANE), BF16),
            vmem((CELL, 2 * ROWS, MODES), BF16),
            vmem((NY, 2 * ROWS, MODES), BF16),
            vmem((NY - 1, 2 * ROWS, MODES), BF16),
            vmem((NY, ROWS, LANE), BF16),
            vmem((NY * CELL - 1, ROWS, LANE), BF16),
            vmem((ROWS, LANE), BF16),
            vmem((GRP, ROWS, LANE), BF16),
            vmem((2 * ROWS, LANE), BF16),
            vmem((NY - 1, 2 * ROWS, LANE), BF16),
            vmem((CELL, 2 * ROWS, LANE), BF16),
            pltpu.SemaphoreType.DMA((9,)),
            pltpu.SemaphoreType.DMA((8,)),
            pltpu.SemaphoreType.DMA((8,)),
        ],
        compiler_params=pltpu.CompilerParams(
            collective_id=0, has_side_effects=True, vmem_limit_bytes=63 * 1024 * 1024
        ),
        name="scatter_step",
    )(*args)


def solution(mesh):
    return jax.shard_map(
        local,
        mesh=mesh,
        in_specs=(
            P(("grp", "body"), None, None),
            P(("grp", "body"), None, None),
            P(("grp", "body"), None, None, None),
            P(),
            P(("grp", "body"), None),
            P("grp"),
            P(("grp", "body"), None, None, None),
            P(("grp", "body"), None, None, None),
            P("grp", None, None, "body", None),
        ),
        out_specs=P(("grp", "body"), None, None),
        check_vma=False,
    )
```

time: 44.7 us -> 39.2 us (0.88)
  Pallas kernels: 43.1 us -> 37.6 us
    pallas_call x1, Pallas kernels: 43.1 us -> 37.6 us  [local(): pl.pallas_call(kernel, out_shape=jax.ShapeDtypeStruct((1, ROWS, 2 * MODES...]
where the time goes in v3:
time: 39.2 us; the launch traced here: 39 us
  Pallas kernels  37.6 us (96%)
  local copies, waits for them, and re-layouts  1.38 us (4%)
    pallas_call x1, Pallas kernels, local(): pl.pallas_call(kernel, out_shape=jax.ShapeDtypeStruct((1, ROWS, 2 * MODES...  37.6 us
    unnamed x1, local copies, waits for them, and re-layouts  1.38 us

profile of v3, /device:TPU:1, one launch (start us, length us, event | category | flops | bytes accessed | tf_op | source)
XLA Modules:
  0.0 39.0 jit_solution(8829808316506916114)
XLA Ops:
  0.0 37.6 %scatter_step.1 = f32[1,16,512]{2,1,0:T(8,128)} custom-call(bf16[1,16,512]{2,1,0:T(8,128)(2,1)} %incident.1, f32[1,16,512]{2,1,0:T(8,128)} %exciting.1, bf16[1,2,256,256]{3,2,1,0:T(8,128)(2,1)} %t_maps.1, bf16[225,2,512]{2,1,0:T(2,128)(2,1)} %table.1, s32[1,32]{1,0:T(1,128)} %offsets.1, s32[32]{0:T(128)} %slots.1, bf16[1,2,256,512]{3,2,1,0:T(8,128)(2,1)} %up_maps.1, ...), custom_call_target="tpu_custom_call" | custom-call | tf_op jit(solution)/shard_map/scatter_step/pallas_call | solution.py:285
  37.6 1.4 %copy.11 = f32[1,16,512]{2,1,0:T(8,128)} copy(f32[1,16,512]{2,1,0:T(8,128)} %scatter_step.1) | data formatting | bytes 65536

commit v4 on v3

--- a/solution.py
+++ b/solution.py
@@ -312,10 +312,10 @@
             pltpu.SemaphoreType.DMA((8,)),
         ],
         compiler_params=pltpu.CompilerParams(
-            collective_id=0, has_side_effects=True, vmem_limit_bytes=63 * 1024 * 1024
+            collective_id=0, has_side_effects=True, vmem_limit_bytes=32 * 1024 * 1024
         ),
         name="scatter_step",
-    )(*args)
+    )(*[pltpu.with_memory_space_constraint(a, pltpu.HBM) for a in args])
 
 
 def solution(mesh):

time: 39.2 us -> 37.8 us (0.964)
  local copies, waits for them, and re-layouts: 1.38 us -> 0.62 us
  Pallas kernels: 37.6 us -> 37 us
    unnamed x1, local copies, waits for them, and re-layouts: 1.38 us -> 0.62 us
    pallas_call x1, Pallas kernels: 37.6 us -> 37 us  [local(): pl.pallas_call(kernel, out_shape=jax.ShapeDtypeStruct((1, ROWS, 2 * MODES...]
where the time goes in v4:
time: 37.8 us; the launch traced here: 37.6 us
  Pallas kernels  37 us (98%)
  local copies, waits for them, and re-layouts  0.62 us (2%)
    pallas_call x1, Pallas kernels, local(): pl.pallas_call(kernel, out_shape=jax.ShapeDtypeStruct((1, ROWS, 2 * MODES...  37 us

profile of v4, /device:TPU:1, one launch (start us, length us, event | category | flops | bytes accessed | tf_op | source)
XLA Modules:
  0.0 37.6 jit_solution(12510842090420250899)
XLA Ops:
  0.0 37.0 %scatter_step.1 = f32[1,16,512]{2,1,0:T(8,128)S(1)} custom-call(bf16[1,16,512]{2,1,0:T(8,128)(2,1)} %incident.1, f32[1,16,512]{2,1,0:T(8,128)} %exciting.1, bf16[1,2,256,256]{3,2,1,0:T(8,128)(2,1)} %t_maps.1, bf16[225,2,512]{2,1,0:T(2,128)(2,1)} %table.1, s32[1,32]{1,0:T(1,128)} %offsets.1, s32[32]{0:T(128)} %slots.1, bf16[1,2,256,512]{3,2,1,0:T(8,128)(2,1)} %up_maps.1, ...), custom_call_target="tpu_custom_call" | custom-call | tf_op jit(solution)/shard_map/scatter_step/pallas_call | solution.py:285
  37.0 0.6 %copy.11 = f32[1,16,512]{2,1,0:T(8,128)} copy(f32[1,16,512]{2,1,0:T(8,128)S(1)} %scatter_step.1) | data formatting | bytes 65536

commit v5 on v4

--- a/solution.py
+++ b/solution.py
@@ -35,12 +35,24 @@
     for dc in (2, 3, 1, 0)
     if (dy, dc) != (0, 0)
 ]
+FAR_BODY = 12
 Y_STEPS = (4, 3, 5, 2, 6, 1, 7)
 CELL_STEPS = (2, 3, 1)
+CORE_STEPS = [(dy, dc) for dy in (4, 3, 5, 2, 6, 1, 7, 0) for dc in (2, 0) if (dy, dc) != (0, 0)]
+FAR_CORE = 6
 GRP_STEPS = sorted(
     [(dx, dz) for dx in range(4) for dz in range(4) if (dx, dz) != (0, 0)],
     key=lambda s: -(min(s[0], 4 - s[0]) + 2 * min(s[1], 4 - s[1])),
 )
+FAR_GRP = 4
+
+
+def grp_hops(step):
+    return min(step[0], 4 - step[0]) + 2 * min(step[1], 4 - step[1])
+
+
+def body_hops(step):
+    return min(step[0], NY - step[0]) + (0, 0.5, 1, 0.5)[step[1]]
 
 
 def kernel(
@@ -87,6 +99,28 @@
     def quarter(member):
         return group_maps.at[0, :, :, :, pl.ds(pl.multiple_of(member * LANE, LANE), LANE)]
 
+    def body_peer(step):
+        dy, dc = step
+        return {"grp": g, "body": lax.rem(y + dy, NY) * CELL + lax.rem(c + dc, CELL)}
+
+    def y_peer(d):
+        return body_peer((d, 0))
+
+    def cell_peer(d):
+        return body_peer((0, d))
+
+    def grp_peer(step):
+        dx, dz = step
+        return {"grp": lax.rem(gx + dx, 4) * 4 + lax.rem(gz + dz, 4), "body": b}
+
+    barrier = pltpu.get_barrier_semaphore()
+    greeted = [(grp_hops(s), grp_peer, s) for s in GRP_STEPS]
+    greeted += [(body_hops(s), body_peer, s) for s in BODY_STEPS]
+    for _, peer, step in sorted(greeted, key=lambda entry: -entry[0]):
+        pl.semaphore_signal(
+            barrier, inc=1, device_id=peer(step), device_id_type=pl.DeviceIdType.MESH
+        )
+
     loads = [
         pltpu.make_async_copy(src, dst, load_sem.at[k])
         for k, (src, dst) in enumerate(
@@ -107,24 +141,6 @@
         copy.start()
     l_inc, l_t, l_up, l_off, l_slot, l_table, l_gm, l_down, l_exc = loads
 
-    def body_peer(step):
-        dy, dc = step
-        return {"grp": g, "body": lax.rem(y + dy, NY) * CELL + lax.rem(c + dc, CELL)}
-
-    def y_peer(d):
-        return body_peer((d, 0))
-
-    def cell_peer(d):
-        return body_peer((0, d))
-
-    def grp_peer(step):
-        dx, dz = step
-        return {"grp": lax.rem(gx + dx, 4) * 4 + lax.rem(gz + dz, 4), "body": b}
-
-    barrier = pltpu.get_barrier_semaphore()
-    for peer in [grp_peer(s) for s in GRP_STEPS] + [body_peer(s) for s in BODY_STEPS]:
-        pl.semaphore_signal(barrier, inc=1, device_id=peer, device_id_type=pl.DeviceIdType.MESH)
-
     def send(src, dst, phase, peer):
         pltpu.make_async_remote_copy(
             src_ref=src,
@@ -162,7 +178,8 @@
 
     pl.semaphore_wait(barrier, len(BODY_STEPS) + len(GRP_STEPS))
     for k, step in enumerate(BODY_STEPS):
-        send(u_out.at[lax.rem(y + step[0], NY)], u_in.at[k], 2, body_peer(step))
+        phase = 2 if k < FAR_BODY else 8
+        send(u_out.at[lax.rem(y + step[0], NY)], u_in.at[k], phase, body_peer(step))
     for d in Y_STEPS:
         send(s_off.at[pl.ds(0, 1)], s_off.at[pl.ds(NY - d, 1)], 0, y_peer(d))
     for d in CELL_STEPS:
@@ -170,13 +187,18 @@
     for d in CELL_STEPS:
         send(quarter(lax.rem(c + d, CELL)), w_gm.at[:, :, c], 3, cell_peer(d))
 
-    wait_recv(u_in, 2)
+    near_body = u_in.at[pl.ds(FAR_BODY, len(BODY_STEPS) - FAR_BODY)]
+    far_body = u_in.at[pl.ds(0, FAR_BODY)]
     e_sum = u_out[y].astype(F32)
-    for k in range(len(BODY_STEPS)):
+    wait_recv(near_body, 8)
+    for k in range(FAR_BODY, len(BODY_STEPS)):
+        e_sum += u_in[k].astype(F32)
+    wait_recv(far_body, 2)
+    for k in range(FAR_BODY):
         e_sum += u_in[k].astype(F32)
     g_out[...] = e_sum.astype(BF16)
     for step in GRP_STEPS:
-        send(g_out, g_in.at[g], 4, grp_peer(step))
+        send(g_out, g_in.at[g], 4 if step[1] == 2 else 9, grp_peer(step))
     g_in[g] = jnp.zeros((ROWS, LANE), BF16)
 
     l_slot.wait()
@@ -232,27 +254,59 @@
 
     l_gm.wait()
     wait_recv(w_gm.at[:, :, pl.ds(0, CELL - 1)], 3)
-    wait_recv(g_in.at[pl.ds(0, GRP - 1)], 4)
-    tops, bottoms = [], []
-    for h in range(GRP):
-        pair = g_in[h].astype(F32)
-        tops.append(jnp.where(low, pair, -pair).astype(BF16))
-        bottoms.append(pltpu.roll(pair, HALF, 1).astype(BF16))
-    left = jnp.concatenate(
-        [jnp.concatenate(tops, axis=1), jnp.concatenate(bottoms, axis=1)], axis=0
-    )
-    p_sum = dot(left, w_gm[...].reshape(GRP * LANE, LANE))
-    p_out[...] = p_sum.astype(BF16)
-    for k, d in enumerate(Y_STEPS):
-        send(p_out, p_in.at[k], 5, y_peer(d))
+
+    def from_groups(z_steps):
+        tops, bottoms, mats = [], [], []
+        for dz in z_steps:
+            for x_at in range(4):
+                h = x_at * 4 + lax.rem(gz + dz, 4)
+                pair = g_in[h].astype(F32)
+                tops.append(jnp.where(low, pair, -pair).astype(BF16))
+                bottoms.append(pltpu.roll(pair, HALF, 1).astype(BF16))
+                mats.append(w_gm[h].reshape(LANE, LANE))
+        left = jnp.concatenate(
+            [jnp.concatenate(tops, axis=1), jnp.concatenate(bottoms, axis=1)], axis=0
+        )
+        return dot(left, jnp.concatenate(mats, axis=0))
+
+    near_grp = g_in.at[pl.ds(0, GRP - 1 - FAR_GRP)]
+    far_grp = g_in.at[pl.ds(0, FAR_GRP)]
+    wait_recv(near_grp, 9)
+    p_own = from_groups((0, 1, 3))
+    wait_recv(far_grp, 4)
+    p_own += from_groups((2,))
+    p_out[...] = p_own.astype(BF16)
+    for k, step in enumerate(CORE_STEPS):
+        send(p_out, p_in.at[k], 5 if k < FAR_CORE else 10, body_peer(step))
 
     near = near_one(0)
-    wait_recv(p_in, 5)
-    for k in range(NY - 1):
-        p_sum += p_in[k].astype(F32)
-    i_all[c] = p_sum.astype(BF16)
-    for d in CELL_STEPS:
-        send(i_all.at[c], i_all.at[c], 7, cell_peer(d))
+    near_core = p_in.at[pl.ds(FAR_CORE, len(CORE_STEPS) - FAR_CORE)]
+    far_core = p_in.at[pl.ds(0, FAR_CORE)]
+
+    def sums(mine, other, low_k, high_k):
+        for k in range(low_k, high_k):
+            if CORE_STEPS[k][1] == 0:
+                mine += p_in[k].astype(F32)
+            else:
+                other += p_in[k].astype(F32)
+        return mine, other
+
+    wait_recv(near_core, 10)
+    mine, other = sums(p_own, jnp.zeros_like(p_own), FAR_CORE, len(CORE_STEPS))
+    wait_recv(far_core, 5)
+    mine, other = sums(mine, other, 0, FAR_CORE)
+    z_at = c // 2
+    core = c % 2
+    i_all[2 * core + z_at] = mine.astype(BF16)
+    i_all[2 * core + 1 - z_at] = other.astype(BF16)
+    pltpu.make_async_remote_copy(
+        src_ref=i_all.at[pl.ds(2 * core, 2)],
+        dst_ref=i_all.at[pl.ds(2 * core, 2)],
+        send_sem=send_sem.at[7],
+        recv_sem=recv_sem.at[7],
+        device_id={"grp": g, "body": y * CELL + z_at * 2 + 1 - core},
+        device_id_type=pl.DeviceIdType.MESH,
+    ).start()
 
     wait_recv(near_in, 6)
     for k in range(NY - 1):
@@ -261,22 +315,33 @@
     near_re = v_exc[:, :MODES] + near[:ROWS]
     near_im = v_exc[:, MODES:] + near[ROWS:]
 
+    def from_core(at):
+        total = jnp.zeros((2 * ROWS, MODES), F32)
+        for z in range(2):
+            tile = i_all[2 * at + z]
+            rows = pl.ds(pl.multiple_of((2 * z + at) * LANE, LANE), LANE)
+            mats = jnp.concatenate([v_down[0, rows, :], v_down[1, rows, :]], axis=0)
+            total += dot(paired(tile[:ROWS], tile[ROWS:]), mats)
+        return total
+
     l_down.wait()
-    wait_recv(i_all.at[pl.ds(0, CELL - 1)], 7)
-    incoming_re = jnp.concatenate([i_all[k][:ROWS] for k in range(CELL)], axis=1)
-    incoming_im = jnp.concatenate([i_all[k][ROWS:] for k in range(CELL)], axis=1)
-    far = dot(paired(incoming_re, incoming_im), v_down[...].reshape(2 * COEFS, MODES))
+    far = from_core(core)
+    wait_recv(i_all.at[pl.ds(0, 2)], 7)
+    far += from_core(1 - core)
     out[0, :, :MODES] = near_re + far[:ROWS]
     out[0, :, MODES:] = near_im + far[ROWS:]
 
     wait_send(s_off.at[pl.ds(0, NY - 1)], 0)
     wait_send(scat.at[pl.ds(0, CELL - 1)], 1)
-    wait_send(u_in, 2)
+    wait_send(far_body, 2)
+    wait_send(near_body, 8)
     wait_send(w_gm.at[:, :, pl.ds(0, CELL - 1)], 3)
-    wait_send(g_in.at[pl.ds(0, GRP - 1)], 4)
-    wait_send(p_in, 5)
+    wait_send(far_grp, 4)
+    wait_send(near_grp, 9)
+    wait_send(far_core, 5)
+    wait_send(near_core, 10)
     wait_send(near_in, 6)
-    wait_send(i_all.at[pl.ds(0, CELL - 1)], 7)
+    wait_send(i_all.at[pl.ds(0, 2)], 7)
 
 
 def local(*args):
@@ -305,11 +370,11 @@
             vmem((ROWS, LANE), BF16),
             vmem((GRP, ROWS, LANE), BF16),
             vmem((2 * ROWS, LANE), BF16),
-            vmem((NY - 1, 2 * ROWS, LANE), BF16),
+            vmem((len(CORE_STEPS), 2 * ROWS, LANE), BF16),
             vmem((CELL, 2 * ROWS, LANE), BF16),
             pltpu.SemaphoreType.DMA((9,)),
-            pltpu.SemaphoreType.DMA((8,)),
-            pltpu.SemaphoreType.DMA((8,)),
+            pltpu.SemaphoreType.DMA((11,)),
+            pltpu.SemaphoreType.DMA((11,)),
         ],
         compiler_params=pltpu.CompilerParams(
             collective_id=0, has_side_effects=True, vmem_limit_bytes=32 * 1024 * 1024

time: 37.8 us -> 36.7 us (0.971)
  Pallas kernels: 37 us -> 35.9 us
    pallas_call x1, Pallas kernels: 37 us -> 35.9 us  [local(): pl.pallas_call(kernel, out_shape=jax.ShapeDtypeStruct((1, ROWS, 2 * MODES...]
where the time goes in v5:
time: 36.7 us; the launch traced here: 36.5 us
  Pallas kernels  35.9 us (98%)
  local copies, waits for them, and re-layouts  0.62 us (2%)
    pallas_call x1, Pallas kernels, local(): pl.pallas_call(kernel, out_shape=jax.ShapeDtypeStruct((1, ROWS, 2 * MODES...  35.9 us

profile of v5, /device:TPU:1, one launch (start us, length us, event | category | flops | bytes accessed | tf_op | source)
XLA Modules:
  0.0 36.5 jit_solution(640044100631563504)
XLA Ops:
  0.0 35.9 %scatter_step.1 = f32[1,16,512]{2,1,0:T(8,128)S(1)} custom-call(bf16[1,16,512]{2,1,0:T(8,128)(2,1)} %incident.1, f32[1,16,512]{2,1,0:T(8,128)} %exciting.1, bf16[1,2,256,256]{3,2,1,0:T(8,128)(2,1)} %t_maps.1, bf16[225,2,512]{2,1,0:T(2,128)(2,1)} %table.1, s32[1,32]{1,0:T(1,128)} %offsets.1, s32[32]{0:T(128)} %slots.1, bf16[1,2,256,512]{3,2,1,0:T(8,128)(2,1)} %up_maps.1, ...), custom_call_target="tpu_custom_call" | custom-call | tf_op jit(solution)/shard_map/scatter_step/pallas_call | solution.py:350
  35.9 0.6 %copy.11 = f32[1,16,512]{2,1,0:T(8,128)} copy(f32[1,16,512]{2,1,0:T(8,128)S(1)} %scatter_step.1) | data formatting | bytes 65536

commit v6 on v5

--- a/solution.py
+++ b/solution.py
@@ -45,6 +45,7 @@
     key=lambda s: -(min(s[0], 4 - s[0]) + 2 * min(s[1], 4 - s[1])),
 )
 FAR_GRP = 4
+EARLY_GRP = 10
 
 
 def grp_hops(step):
@@ -96,8 +97,9 @@
     gx = g // 4
     gz = g % 4
 
-    def quarter(member):
-        return group_maps.at[0, :, :, :, pl.ds(pl.multiple_of(member * LANE, LANE), LANE)]
+    def quarter(member, low_h=0, high_h=GRP):
+        columns = pl.ds(pl.multiple_of(member * LANE, LANE), LANE)
+        return group_maps.at[0, pl.ds(low_h, high_h - low_h), :, :, columns]
 
     def body_peer(step):
         dy, dc = step
@@ -157,6 +159,15 @@
     def wait_send(ref, phase):
         pltpu.make_async_copy(ref, ref, send_sem.at[phase]).wait()
 
+    def send_weights(low_h, high_h):
+        for d in CELL_STEPS:
+            send(
+                quarter(lax.rem(c + d, CELL), low_h, high_h),
+                w_gm.at[pl.ds(low_h, high_h - low_h), :, c],
+                3,
+                cell_peer(d),
+            )
+
     l_inc.wait()
     l_t.wait()
     x = v_inc[...]
@@ -184,8 +195,7 @@
         send(s_off.at[pl.ds(0, 1)], s_off.at[pl.ds(NY - d, 1)], 0, y_peer(d))
     for d in CELL_STEPS:
         send(scat.at[c], scat.at[c], 1, cell_peer(d))
-    for d in CELL_STEPS:
-        send(quarter(lax.rem(c + d, CELL)), w_gm.at[:, :, c], 3, cell_peer(d))
+    send_weights(0, EARLY_GRP)
 
     near_body = u_in.at[pl.ds(FAR_BODY, len(BODY_STEPS) - FAR_BODY)]
     far_body = u_in.at[pl.ds(0, FAR_BODY)]
@@ -200,6 +210,7 @@
     for step in GRP_STEPS:
         send(g_out, g_in.at[g], 4 if step[1] == 2 else 9, grp_peer(step))
     g_in[g] = jnp.zeros((ROWS, LANE), BF16)
+    send_weights(EARLY_GRP, GRP)
 
     l_slot.wait()
     l_table.wait()

time: 36.7 us -> 35.6 us (0.970)
  Pallas kernels: 35.9 us -> 34.9 us
    pallas_call x1, Pallas kernels: 35.9 us -> 34.9 us  [local(): pl.pallas_call(kernel, out_shape=jax.ShapeDtypeStruct((1, ROWS, 2 * MODES...]
where the time goes in v6:
time: 35.6 us; the launch traced here: 35.5 us
  Pallas kernels  34.9 us (98%)
  local copies, waits for them, and re-layouts  0.62 us (2%)
    pallas_call x1, Pallas kernels, local(): pl.pallas_call(kernel, out_shape=jax.ShapeDtypeStruct((1, ROWS, 2 * MODES...  34.9 us

profile of v6, /device:TPU:1, one launch (start us, length us, event | category | flops | bytes accessed | tf_op | source)
XLA Modules:
  0.0 35.5 jit_solution(7470214398812653218)
XLA Ops:
  0.0 34.9 %scatter_step.1 = f32[1,16,512]{2,1,0:T(8,128)S(1)} custom-call(bf16[1,16,512]{2,1,0:T(8,128)(2,1)} %incident.1, f32[1,16,512]{2,1,0:T(8,128)} %exciting.1, bf16[1,2,256,256]{3,2,1,0:T(8,128)(2,1)} %t_maps.1, bf16[225,2,512]{2,1,0:T(2,128)(2,1)} %table.1, s32[1,32]{1,0:T(1,128)} %offsets.1, s32[32]{0:T(128)} %slots.1, bf16[1,2,256,512]{3,2,1,0:T(8,128)(2,1)} %up_maps.1, ...), custom_call_target="tpu_custom_call" | custom-call | tf_op jit(solution)/shard_map/scatter_step/pallas_call | solution.py:361
  34.9 0.6 %copy.11 = f32[1,16,512]{2,1,0:T(8,128)} copy(f32[1,16,512]{2,1,0:T(8,128)S(1)} %scatter_step.1) | data formatting | bytes 65536

commit v7 on v6

--- a/solution.py
+++ b/solution.py
@@ -29,7 +29,7 @@
     )
 
 
-BODY_STEPS = [
+Y_STEPS = [
     (dy, dc)
     for dy in (4, 3, 5, 2, 6, 1, 7, 0)
     for dc in (2, 3, 1, 0)
@@ -40,6 +40,7 @@
 CELL_STEPS = (2, 3, 1)
 CORE_STEPS = [(dy, dc) for dy in (4, 3, 5, 2, 6, 1, 7, 0) for dc in (2, 0) if (dy, dc) != (0, 0)]
 FAR_CORE = 6
+BODY_STEPS = [*CORE_STEPS, (0, 1), (0, 3)]
 GRP_STEPS = sorted(
     [(dx, dz) for dx in range(4) for dz in range(4) if (dx, dz) != (0, 0)],
     key=lambda s: -(min(s[0], 4 - s[0]) + 2 * min(s[1], 4 - s[1])),
@@ -81,6 +82,8 @@
     near_in,
     u_out,
     u_in,
+    e_out,
+    e_in,
     g_out,
     g_in,
     p_out,
@@ -188,8 +191,8 @@
     l_off.wait()
 
     pl.semaphore_wait(barrier, len(BODY_STEPS) + len(GRP_STEPS))
-    for k, step in enumerate(BODY_STEPS):
-        phase = 2 if k < FAR_BODY else 8
+    for k, step in enumerate(CORE_STEPS):
+        phase = 2 if k < FAR_CORE else 8
         send(u_out.at[lax.rem(y + step[0], NY)], u_in.at[k], phase, body_peer(step))
     for d in Y_STEPS:
         send(s_off.at[pl.ds(0, 1)], s_off.at[pl.ds(NY - d, 1)], 0, y_peer(d))
@@ -197,15 +200,22 @@
         send(scat.at[c], scat.at[c], 1, cell_peer(d))
     send_weights(0, EARLY_GRP)
 
-    near_body = u_in.at[pl.ds(FAR_BODY, len(BODY_STEPS) - FAR_BODY)]
-    far_body = u_in.at[pl.ds(0, FAR_BODY)]
+    near_body = u_in.at[pl.ds(FAR_CORE, len(CORE_STEPS) - FAR_CORE)]
+    far_body = u_in.at[pl.ds(0, FAR_CORE)]
     e_sum = u_out[y].astype(F32)
     wait_recv(near_body, 8)
-    for k in range(FAR_BODY, len(BODY_STEPS)):
+    for k in range(FAR_CORE, len(CORE_STEPS)):
         e_sum += u_in[k].astype(F32)
     wait_recv(far_body, 2)
-    for k in range(FAR_BODY):
+    for k in range(FAR_CORE):
         e_sum += u_in[k].astype(F32)
+    e_out[...] = e_sum
+    z_at = c // 2
+    core = c % 2
+    other_core = {"grp": g, "body": y * CELL + z_at * 2 + 1 - core}
+    send(e_out, e_in, 11, other_core)
+    wait_recv(e_in, 11)
+    e_sum += e_in[...]
     g_out[...] = e_sum.astype(BF16)
     for step in GRP_STEPS:
         send(g_out, g_in.at[g], 4 if step[1] == 2 else 9, grp_peer(step))
@@ -306,18 +316,10 @@
     mine, other = sums(p_own, jnp.zeros_like(p_own), FAR_CORE, len(CORE_STEPS))
     wait_recv(far_core, 5)
     mine, other = sums(mine, other, 0, FAR_CORE)
-    z_at = c // 2
-    core = c % 2
     i_all[2 * core + z_at] = mine.astype(BF16)
     i_all[2 * core + 1 - z_at] = other.astype(BF16)
-    pltpu.make_async_remote_copy(
-        src_ref=i_all.at[pl.ds(2 * core, 2)],
-        dst_ref=i_all.at[pl.ds(2 * core, 2)],
-        send_sem=send_sem.at[7],
-        recv_sem=recv_sem.at[7],
-        device_id={"grp": g, "body": y * CELL + z_at * 2 + 1 - core},
-        device_id_type=pl.DeviceIdType.MESH,
-    ).start()
+    pair_of_core = i_all.at[pl.ds(2 * core, 2)]
+    send(pair_of_core, pair_of_core, 7, other_core)
 
     wait_recv(near_in, 6)
     for k in range(NY - 1):
@@ -346,6 +348,7 @@
     wait_send(scat.at[pl.ds(0, CELL - 1)], 1)
     wait_send(far_body, 2)
     wait_send(near_body, 8)
+    wait_send(e_in, 11)
     wait_send(w_gm.at[:, :, pl.ds(0, CELL - 1)], 3)
     wait_send(far_grp, 4)
     wait_send(near_grp, 9)
@@ -377,15 +380,17 @@
             vmem((NY, 2 * ROWS, MODES), BF16),
             vmem((NY - 1, 2 * ROWS, MODES), BF16),
             vmem((NY, ROWS, LANE), BF16),
-            vmem((NY * CELL - 1, ROWS, LANE), BF16),
+            vmem((len(CORE_STEPS), ROWS, LANE), BF16),
+            vmem((ROWS, LANE), F32),
+            vmem((ROWS, LANE), F32),
             vmem((ROWS, LANE), BF16),
             vmem((GRP, ROWS, LANE), BF16),
             vmem((2 * ROWS, LANE), BF16),
             vmem((len(CORE_STEPS), 2 * ROWS, LANE), BF16),
             vmem((CELL, 2 * ROWS, LANE), BF16),
             pltpu.SemaphoreType.DMA((9,)),
-            pltpu.SemaphoreType.DMA((11,)),
-            pltpu.SemaphoreType.DMA((11,)),
+            pltpu.SemaphoreType.DMA((12,)),
+            pltpu.SemaphoreType.DMA((12,)),
         ],
         compiler_params=pltpu.CompilerParams(
             collective_id=0, has_side_effects=True, vmem_limit_bytes=32 * 1024 * 1024

time: 35.6 us -> 35.4 us (level)
  no operation moved by 1% of the time
where the time goes in v7:
time: 35.4 us; the launch traced here: 35.2 us
  Pallas kernels  34.6 us (98%)
  local copies, waits for them, and re-layouts  0.62 us (2%)
    pallas_call x1, Pallas kernels, local(): pl.pallas_call(kernel, out_shape=jax.ShapeDtypeStruct((1, ROWS, 2 * MODES...  34.6 us

profile of v7, /device:TPU:1, one launch (start us, length us, event | category | flops | bytes accessed | tf_op | source)
XLA Modules:
  0.0 35.2 jit_solution(3614890206188720437)
XLA Ops:
  0.0 34.6 %scatter_step.1 = f32[1,16,512]{2,1,0:T(8,128)S(1)} custom-call(bf16[1,16,512]{2,1,0:T(8,128)(2,1)} %incident.1, f32[1,16,512]{2,1,0:T(8,128)} %exciting.1, bf16[1,2,256,256]{3,2,1,0:T(8,128)(2,1)} %t_maps.1, bf16[225,2,512]{2,1,0:T(2,128)(2,1)} %table.1, s32[1,32]{1,0:T(1,128)} %offsets.1, s32[32]{0:T(128)} %slots.1, bf16[1,2,256,512]{3,2,1,0:T(8,128)(2,1)} %up_maps.1, ...), custom_call_target="tpu_custom_call" | custom-call | tf_op jit(solution)/shard_map/scatter_step/pallas_call | solution.py:364
  34.6 0.6 %copy.11 = f32[1,16,512]{2,1,0:T(8,128)} copy(f32[1,16,512]{2,1,0:T(8,128)S(1)} %scatter_step.1) | data formatting | bytes 65536

commit v8 on v7

--- a/solution.py
+++ b/solution.py
@@ -118,14 +118,6 @@
         dx, dz = step
         return {"grp": lax.rem(gx + dx, 4) * 4 + lax.rem(gz + dz, 4), "body": b}
 
-    barrier = pltpu.get_barrier_semaphore()
-    greeted = [(grp_hops(s), grp_peer, s) for s in GRP_STEPS]
-    greeted += [(body_hops(s), body_peer, s) for s in BODY_STEPS]
-    for _, peer, step in sorted(greeted, key=lambda entry: -entry[0]):
-        pl.semaphore_signal(
-            barrier, inc=1, device_id=peer(step), device_id_type=pl.DeviceIdType.MESH
-        )
-
     loads = [
         pltpu.make_async_copy(src, dst, load_sem.at[k])
         for k, (src, dst) in enumerate(
@@ -142,9 +134,19 @@
             ]
         )
     ]
-    for copy in loads:
+    l_inc, l_t, l_up, l_off, l_slot, l_table, l_gm, l_down, l_exc = loads
+    for copy in loads[:3]:
         copy.start()
-    l_inc, l_t, l_up, l_off, l_slot, l_table, l_gm, l_down, l_exc = loads
+    barrier = pltpu.get_barrier_semaphore()
+    greeted = [(grp_hops(s), grp_peer, s) for s in GRP_STEPS]
+    greeted += [(body_hops(s), body_peer, s) for s in BODY_STEPS]
+    for _, peer, step in sorted(greeted, key=lambda entry: -entry[0]):
+        pl.semaphore_signal(
+            barrier, inc=1, device_id=peer(step), device_id_type=pl.DeviceIdType.MESH
+        )
+
+    for copy in loads[3:]:
+        copy.start()
 
     def send(src, dst, phase, peer):
         pltpu.make_async_remote_copy(

time: 35.4 us -> 35.4 us (level)
  no operation moved by 1% of the time
where the time goes in v8:
time: 35.4 us; the launch traced here: 35.2 us
  Pallas kernels  34.6 us (98%)
  local copies, waits for them, and re-layouts  0.62 us (2%)
    pallas_call x1, Pallas kernels, local(): pl.pallas_call(kernel, out_shape=jax.ShapeDtypeStruct((1, ROWS, 2 * MODES...  34.6 us

profile of v8, /device:TPU:1, one launch (start us, length us, event | category | flops | bytes accessed | tf_op | source)
XLA Modules:
  0.0 35.2 jit_solution(16764837682549991978)
XLA Ops:
  0.0 34.6 %scatter_step.1 = f32[1,16,512]{2,1,0:T(8,128)S(1)} custom-call(bf16[1,16,512]{2,1,0:T(8,128)(2,1)} %incident.1, f32[1,16,512]{2,1,0:T(8,128)} %exciting.1, bf16[1,2,256,256]{3,2,1,0:T(8,128)(2,1)} %t_maps.1, bf16[225,2,512]{2,1,0:T(2,128)(2,1)} %table.1, s32[1,32]{1,0:T(1,128)} %offsets.1, s32[32]{0:T(128)} %slots.1, bf16[1,2,256,512]{3,2,1,0:T(8,128)(2,1)} %up_maps.1, ...), custom_call_target="tpu_custom_call" | custom-call | tf_op jit(solution)/shard_map/scatter_step/pallas_call | solution.py:366
  34.6 0.6 %copy.11 = f32[1,16,512]{2,1,0:T(8,128)} copy(f32[1,16,512]{2,1,0:T(8,128)S(1)} %scatter_step.1) | data formatting | bytes 65536
